TPU v7x, 32 devices: a whole 2x2x4 slice. The times are simulated.
32 devices in a mesh: groups: 2 (over y), seq: 4 (over z), dp: 2 (over x), sub: 2 (over core).
Axes of the slice: x: 2, y: 2, z: 4, core: 2. Of those that a mesh axis runs over, the one named last changes fastest.
Arguments:
- signal: bfloat16 [8, 2048, 512], P(('groups', 'dp', 'sub'), 'seq'), parts along dimension 0, may hold values from -6 to 6
- conv_weight: bfloat16 [512, 3, 1024], P(('dp', 'sub')), may hold values from -0.15625 to 0.15625
- proj_weight: bfloat16 [512, 512], P(('dp', 'sub')), may hold values from -0.25 to 0.25
- cotangent: bfloat16 [8, 2048, 512], P(('groups', 'dp', 'sub'), 'seq'), parts along dimension 0, may hold values from -6 to 6
Outputs:
- output: bfloat16 [8, 2048, 512], P(('groups', 'dp', 'sub'), 'seq'), parts along dimension 0
- grad_input: bfloat16 [8, 2048, 512], P(('groups', 'dp', 'sub'), 'seq'), parts along dimension 0
- grad_conv: float32 [1024, 3, 1024], P(('groups', 'dp', 'sub')), parts along dimension 0
- grad_proj: float32 [1024, 512], P(('groups', 'dp', 'sub')), parts along dimension 0
There are 2 independent parts, one for each index of `groups`. A program takes and returns all parts, laid end to end along the dimension named above; an argument that names none is the same for every part. Nothing has to cross between parts.
All inputs are finite; a program needn't handle non-finite values.
Results may differ from a plain program's by a relative error of at most 0.012.
Values may be sent and summed in bfloat16 or wider, within the bound.
A program may use at most 64 MiB of HBM per device.

v0:
```python
import math
import jax
import jax.numpy as jnp
from jax import lax
from jax.sharding import PartitionSpec as P

DILATION = 512


def passed_along(block, axis, distance):
    devices = range(lax.axis_size(axis))
    route = [(i - distance, i) for i in devices if i - distance in devices]
    return lax.ppermute(block, axis, route)


def relay_earlier(block, reach_blocks):
    blocks = [block]
    current = block
    for step_index in range(reach_blocks):
        current = passed_along(current, "seq", 1)
        blocks.append(current)
    return jnp.concatenate(blocks[::-1], axis=0)


def relay_later(block, reach_blocks):
    blocks = [block]
    current = block
    for step_index in range(reach_blocks):
        current = passed_along(current, "seq", -1)
        blocks.append(current)
    return jnp.concatenate(blocks, axis=0)


def local(signal, conv_weight, proj_weight, cotangent):
    signal_block = signal[0]
    upstream = cotangent[0]
    row_count, channels = signal_block.shape
    offsets = [tap_index * DILATION for tap_index in range(3)]
    reach_blocks = (2 * DILATION + row_count - 1) // row_count
    full_conv = lax.all_gather(conv_weight, ("dp", "sub"), axis=0, tiled=True)
    full_proj = lax.all_gather(proj_weight, ("dp", "sub"), axis=0, tiled=True)
    window = relay_earlier(signal_block, reach_blocks)
    base_row = reach_blocks * row_count
    taps = [window[base_row - offset : base_row - offset + row_count] for offset in offsets]
    preact = jnp.dot(taps[0], full_conv[:, 0, :], preferred_element_type=jnp.float32)
    for tap_index in range(1, 3):
        preact = preact + jnp.dot(
            taps[tap_index], full_conv[:, tap_index, :], preferred_element_type=jnp.float32
        )
    tanh_part = jnp.tanh(preact[:, :channels])
    gate_part = jax.nn.sigmoid(preact[:, channels:])
    gated = (tanh_part * gate_part).astype(jnp.bfloat16)
    output = (
        signal_block.astype(jnp.float32)
        + jnp.dot(gated, full_proj, preferred_element_type=jnp.float32)
    ).astype(jnp.bfloat16)
    transposed = (((1,), (1,)), ((), ()))
    grad_gated = lax.dot_general(
        upstream,
        lax.all_gather(proj_weight, ("dp", "sub"), axis=0, tiled=True),
        transposed,
        preferred_element_type=jnp.float32,
    )
    grad_pre = jnp.concatenate(
        [
            grad_gated * gate_part * (1.0 - tanh_part * tanh_part),
            grad_gated * tanh_part * gate_part * (1.0 - gate_part),
        ],
        axis=1,
    ).astype(jnp.bfloat16)
    ahead_window = relay_later(grad_pre, reach_blocks)
    futures = [ahead_window[offset : offset + row_count] for offset in offsets]
    panel = lax.all_gather(conv_weight, ("dp", "sub"), axis=0, tiled=True)
    summed = lax.dot_general(
        futures[0], panel[:, 0, :], transposed, preferred_element_type=jnp.float32
    )
    for tap_index in range(1, 3):
        summed = summed + lax.dot_general(
            futures[tap_index],
            panel[:, tap_index, :],
            transposed,
            preferred_element_type=jnp.float32,
        )
    grad_input = (upstream.astype(jnp.float32) + summed).astype(jnp.bfloat16)
    outer = (((0,), (0,)), ((), ()))
    terms = [
        lax.dot_general(taps[tap_index], grad_pre, outer, preferred_element_type=jnp.float32)
        for tap_index in range(3)
    ]
    conv_share = lax.psum_scatter(
        jnp.stack(terms, axis=1).astype(jnp.bfloat16),
        ("dp", "sub"),
        scatter_dimension=0,
        tiled=True,
    )
    proj_share = lax.psum_scatter(
        lax.dot_general(gated, upstream, outer, preferred_element_type=jnp.float32).astype(
            jnp.bfloat16
        ),
        ("dp", "sub"),
        scatter_dimension=0,
        tiled=True,
    )
    conv_total, proj_total = (
        lax.psum(conv_share, "seq").astype(jnp.float32),
        lax.psum(proj_share, "seq").astype(jnp.float32),
    )
    all_rows = row_count * lax.axis_size("seq") * lax.axis_size(("dp", "sub"))
    factor = 1.0 / math.sqrt(all_rows)
    return (output[None], grad_input[None], conv_total * factor, proj_total * factor)


def solution(mesh):
    placed = (
        P(("groups", "dp", "sub"), "seq", None),
        P(("dp", "sub"), None, None),
        P(("dp", "sub"), None),
        P(("groups", "dp", "sub"), "seq", None),
    )
    return jax.shard_map(
        local,
        mesh=mesh,
        in_specs=placed,
        out_specs=(
            P(("groups", "dp", "sub"), "seq", None),
            P(("groups", "dp", "sub"), "seq", None),
            P(("groups", "dp", "sub"), None, None),
            P(("groups", "dp", "sub"), None),
        ),
        check_vma=False,
    )
```

profile of v0, /device:TPU:0, one launch (start us, length us, event | category | flops | bytes accessed | tf_op | source)
XLA Modules:
  0.0 176.0 jit_solution(7137187538387217942)
XLA Ops:
  7.2 0.0 all-gather.2.cloned.1.call-start
  7.2 0.7 all-gather.2.cloned.1.call-update
  7.9 0.0 reduce-scatter.7.cloned.1.call-start
  7.9 5.0 %collective-permute-start = (bf16[512,512]{1,0:T(8,128)(2,1)}, bf16[512,512]{1,0:T(8,128)(2,1)S(1)}, u32[]{:S(2)}, u32[]{:S(2)}) collective-permute-start(bf16[512,512]{1,0:T(8,128)(2,1)} %bitcast.57), channel_id=1, source_target_pairs={{0,4},{4,8},{8,12},{1,5},{5,9},{9,13},{2,6},{6,10},{10,14},{3,7},{... | collective-permute-start | bytes 1572872 | tf_op jit(solution)/shard_map/ppermute | solution.py:13
  12.9 7.4 %all_gather.9 = bf16[512,512]{1,0:T(8,128)(2,1)S(1)} all-gather(bf16[128,512]{1,0:T(8,128)(2,1)} %param.6), channel_id=1, replica_groups=mesh['groups'=2,'seq'=4,'dp'=2,'sub'=2] {'dp','sub'}, dimensions={0}, use_global_device_ids=true | all-gather | bytes 655360 | tf_op jit(solution)/shard_map/all_gather | solution.py:41
  20.3 0.0 copy-start.3
  20.3 4.1 %collective-permute-done = bf16[512,512]{1,0:T(8,128)(2,1)S(1)} collective-permute-done((bf16[512,512]{1,0:T(8,128)(2,1)}, bf16[512,512]{1,0:T(8,128)(2,1)S(1)}, u32[]{:S(2)}, u32[]{:S(2)}) %collective-permute-start) | collective-permute-done | bytes 524320 | tf_op jit(solution)/shard_map/ppermute | solution.py:13
  24.4 4.3 %collective-permute-start.1 = (bf16[512,512]{1,0:T(8,128)(2,1)S(1)}, bf16[512,512]{1,0:T(8,128)(2,1)S(1)}, u32[]{:S(2)}, u32[]{:S(2)}) collective-permute-start(bf16[512,512]{1,0:T(8,128)(2,1)S(1)} %collective-permute-done), channel_id=1, source_target_pairs={{0,4},{4,8},{8,12},{1,5},{5,9},{9,13},{2,6},{6,10},{10,14},{3,7},{... | collective-permute-start | bytes 1572872 | tf_op jit(solution)/shard_map/ppermute | solution.py:13
  28.7 12.2 %all-gather.2.cloned.1.call-done = bf16[512,3,1024]{2,0,1:T(8,128)(2,1)} async-done(((bf16[128,3,1024]{2,0,1:T(8,128)(2,1)}), bf16[512,3,1024]{2,0,1:T(8,128)(2,1)}) %all-gather.2.cloned.1.call-update) | async-done | bytes 3145744 | tf_op jit(solution)/shard_map/all_gather | solution.py:40
  40.8 0.0 copy-start
  40.8 2.2 %fusion.12 = f32[512,1024]{1,0:T(8,128)S(1)} fusion(bf16[512,3,1024]{2,0,1:T(8,128)(2,1)} %all-gather.2.cloned.1.call-done, bf16[1,512,512]{2,1,0:T(8,128)(2,1)} %param.4), kind=kOutput, calls=%fused_computation.31 | convolution fusion | flops 536870912 | bytes 3670016 | tf_op jit(solution)/shard_map/dot_general | solution.py:45
  43.1 0.1 copy-done
  43.2 0.7 fusion.13
  43.9 0.0 copy-start.10
  43.9 0.0 collective-permute-done.1
  44.0 0.8 add_add_fusion
  44.7 0.0 copy-done.3
  44.7 0.2 copy-done.10
  45.0 0.0 copy-start.2
  45.0 1.7 multiply_convert_fusion.1
  46.7 0.0 copy-start.4
  46.7 0.0 copy-done.2
  46.7 0.7 fusion.1
  47.4 0.7 fusion.3
  48.2 0.0 copy-done.4
  48.2 0.0 copy-done.6
  48.2 0.7 fusion.2
  49.0 0.3 pad_maximum_fusion
  49.3 3.1 %copy.17 = bf16[512,3072]{1,0:T(8,128)(2,1)} copy(bf16[512,3072]{0,1:T(8,128)(2,1)S(1)} %bitcast.55) | data formatting | bytes 6291456
  52.4 0.0 copy-start.5
  52.4 0.0 copy-start.7
  52.4 0.0 copy-start.8
  52.4 0.0 reduce-scatter.7.cloned.1.call-update
  52.4 0.0 reduce-scatter.5.cloned.1.call-start
  52.4 1.0 copy-done.5
  53.4 0.2 copy-done.7
  53.6 1.1 pad_maximum_fusion.1
  54.7 1.3 collective-permute-start.2
  56.0 0.0 copy-done.8
  56.0 0.0 copy-done.11
  56.0 1.3 convolution_convert_fusion.3
  57.3 0.0 reduce-scatter.5.cloned.1.call-update
  57.3 0.0 copy-start.1
  57.3 0.0 all-reduce.3.cloned.1.call-start
  57.3 24.9 %collective-permute-done.2 = bf16[512,1024]{1,0:T(8,128)(2,1)} collective-permute-done((bf16[512,1024]{1,0:T(8,128)(2,1)}, bf16[512,1024]{1,0:T(8,128)(2,1)}, u32[]{:S(2)}, u32[]{:S(2)}) %collective-permute-start.2) | collective-permute-done | bytes 1048608 | tf_op jit(solution)/shard_map/ppermute | solution.py:13
  82.2 1.3 collective-permute-start.3
  83.5 2.6 %fusion.7 = bf16[1,512,512]{2,1,0:T(8,128)(2,1)} fusion(bf16[512,512]{1,0:T(8,128)(2,1)} %get-tuple-element.16, bf16[512,512]{1,0:T(8,128)(2,1)} %copy-done.3, bf16[1,512,512]{2,1,0:T(8,128)(2,1)} %param.4), kind=kOutput, calls=%fused_computation.17 | convolution fusion | flops 269221888 | bytes 2097152 | tf_op jit(solution)/shard_map/dot_general | solution.py:55
  86.1 4.4 %reduce-scatter.7.cloned.1.call-done = bf16[128,3072]{1,0:T(8,128)(2,1)} async-done(((bf16[512,3072]{1,0:T(8,128)(2,1)}), bf16[128,3072]{1,0:T(8,128)(2,1)}) %reduce-scatter.7.cloned.1.call-update) | async-done | bytes 786448
  90.5 2.3 %copy.18 = bf16[128,3072]{0,1:T(8,128)(2,1)} copy(bf16[128,3072]{1,0:T(8,128)(2,1)} %reduce-scatter.7.cloned.1.call-done) | data formatting | bytes 1572864
  92.8 22.1 %reduce-scatter.5.cloned.1.call-done = bf16[128,512]{1,0:T(8,128)(2,1)} async-done(((bf16[512,512]{1,0:T(8,128)(2,1)}), bf16[128,512]{1,0:T(8,128)(2,1)}) %reduce-scatter.5.cloned.1.call-update) | async-done | bytes 131088 | tf_op jit(solution)/shard_map/reduce_scatter | solution.py:96
  114.9 0.0 all-reduce.3.cloned.1.call-update
  114.9 0.0 copy-done.1
  114.9 1.9 %fusion.11 = f32[512,512]{1,0:T(8,128)S(1)} fusion(bf16[512,3,1024]{2,0,1:T(8,128)(2,1)S(1)} %copy-done.1, bf16[512,512]{1,0:T(8,128)(2,1)} %copy-done.6, bf16[512,512]{1,0:T(8,128)(2,1)} %copy-done.4), kind=kOutput, calls=%fused_computation.30 | convolution fusion | flops 538968064 | bytes 3145728 | tf_op jit(solution)/shard_map/dot_general | solution.py:74
  116.8 0.0 copy-start.12
  116.9 2.0 %convolution_add_fusion.1 = f32[512,512]{1,0:T(8,128)S(1)} fusion(f32[512,512]{1,0:T(8,128)S(1)} %fusion.11, bf16[512,1024]{1,0:T(8,128)(2,1)} %collective-permute-done.2, bf16[512,3,1024]{2,0,1:T(8,128)(2,1)S(1)} %copy-done.1), kind=kOutput, calls=%fused_computation.8 | convolution fusion | flops 537133056 | bytes 4194304 | tf_op jit(solution)/shard_map/dot_general | solution.py:78
  118.9 0.0 collective-permute-done.3
  118.9 0.0 copy-done.12
  118.9 2.8 %fusion.6 = bf16[1,512,512]{2,1,0:T(8,128)(2,1)} fusion(f32[512,512]{1,0:T(8,128)S(1)} %convolution_add_fusion.1, bf16[512,1024]{1,0:T(8,128)(2,1)} %collective-permute-done.3, bf16[512,3,1024]{2,0,1:T(8,128)(2,1)S(1)} %copy-done.1, bf16[1,512,512]{2,1,0:T(8,128)(2,1)S(1)} %copy-done.12), kind=kOutput, calls=%fused_computation.16 | convolution fusion | flops 537919488 | bytes 4194304 | tf_op jit(solution)/shard_map/dot_general | solution.py:78
  121.7 44.2 %all-reduce.3.cloned.1.call-done = (bf16[128,3,1024]{0,2,1:T(8,128)(2,1)}, bf16[128,512]{1,0:T(8,128)(2,1)}) async-done(((bf16[128,3,1024]{0,2,1:T(8,128)(2,1)}, bf16[128,512]{1,0:T(8,128)(2,1)}), (bf16[128,3,1024]{0,2,1:T(8,128)(2,1)}, bf16[128,512]{1,0:T(8,128)(2,1)})) %all-reduce.3.cloned.1.call-update) | async-done | bytes 917520 | tf_op jit(solution)/shard_map/psum | solution.py:105
  165.9 1.3 convert_multiply_fusion
  167.2 0.0 copy-start.9
  167.2 1.6 copy.13
  168.8 0.0 copy-done.9
  168.8 0.7 convert_multiply_fusion.1
  (2 shorter events, 0.0 us)
Async XLA Ops:
  7.2 33.7 %all-gather.2.cloned.1.call-start = ((), (), s32[]{:S(2)}) async-start(), calls=%async_computation.2 | async-start | bytes 3932160 | tf_op jit(solution)/shard_map/all_gather | solution.py:40
  7.9 82.6 %reduce-scatter.7.cloned.1.call-start = ((), (), s32[]{:S(2)}) async-start(), calls=%async_computation.4 | async-start | bytes 3932160
  7.9 16.4 %collective-permute-start = (bf16[512,512]{1,0:T(8,128)(2,1)}, bf16[512,512]{1,0:T(8,128)(2,1)S(1)}, u32[]{:S(2)}, u32[]{:S(2)}) collective-permute-start(bf16[512,512]{1,0:T(8,128)(2,1)} %bitcast.57), channel_id=1, source_target_pairs={{0,4},{4,8},{8,12},{1,5},{5,9},{9,13},{2,6},{6,10},{10,14},{3,7},{... | collective-permute-start | bytes 1572872 | tf_op jit(solution)/shard_map/ppermute | solution.py:13
  20.3 24.4 %copy-start.3 = (bf16[512,512]{1,0:T(8,128)(2,1)}, bf16[512,512]{1,0:T(8,128)(2,1)S(1)}, u32[]{:S(2)}) copy-start(bf16[512,512]{1,0:T(8,128)(2,1)S(1)} %all_gather.9) | copy-start | bytes 1572868
  24.4 19.6 %collective-permute-start.1 = (bf16[512,512]{1,0:T(8,128)(2,1)S(1)}, bf16[512,512]{1,0:T(8,128)(2,1)S(1)}, u32[]{:S(2)}, u32[]{:S(2)}) collective-permute-start(bf16[512,512]{1,0:T(8,128)(2,1)S(1)} %collective-permute-done), channel_id=1, source_target_pairs={{0,4},{4,8},{8,12},{1,5},{5,9},{9,13},{2,6},{6,10},{10,14},{3,7},{... | collective-permute-start | bytes 1572872 | tf_op jit(solution)/shard_map/ppermute | solution.py:13
  40.8 2.4 %copy-start = (bf16[512,3,1024]{2,0,1:T(8,128)(2,1)S(1)}, bf16[512,3,1024]{2,0,1:T(8,128)(2,1)}, u32[]{:S(2)}) copy-start(bf16[512,3,1024]{2,0,1:T(8,128)(2,1)} %all-gather.2.cloned.1.call-done) | copy-start | bytes 9437188
  43.9 1.0 copy-start.10
  45.0 1.7 copy-start.2
  46.7 1.5 copy-start.4
  46.7 1.5 copy-start.6
  52.4 1.0 copy-start.5
  52.4 1.2 copy-start.7
  52.4 3.6 %copy-start.8 = (bf16[512,512]{1,0:T(8,128)(2,1)S(1)}, bf16[512,512]{1,0:T(8,128)(2,1)}, u32[]{:S(2)}) copy-start(bf16[512,512]{1,0:T(8,128)(2,1)} %get-tuple-element.16) | copy-start | bytes 1572868
  52.4 3.6 %copy-start.11 = (bf16[1,512,512]{2,1,0:T(8,128)(2,1)S(1)}, bf16[1,512,512]{2,1,0:T(8,128)(2,1)}, u32[]{:S(2)}) copy-start(bf16[1,512,512]{2,1,0:T(8,128)(2,1)} %param.7) | copy-start | bytes 1572868
  52.4 62.5 %reduce-scatter.5.cloned.1.call-start = ((), (), s32[]{:S(2)}) async-start(), calls=%async_computation.3 | async-start | bytes 655360 | tf_op jit(solution)/shard_map/reduce_scatter | solution.py:96
  54.7 27.5 %collective-permute-start.2 = (bf16[512,1024]{1,0:T(8,128)(2,1)}, bf16[512,1024]{1,0:T(8,128)(2,1)}, u32[]{:S(2)}, u32[]{:S(2)}) collective-permute-start(bf16[512,1024]{1,0:T(8,128)(2,1)} %pad_maximum_fusion.1), channel_id=1, source_target_pairs={{4,0},{8,4},{12,8},{5,1},{9,5},{13,9},{6,2},{10,6},{14,10},{7,3},{... | collective-permute-start | bytes 3145736 | tf_op jit(solution)/shard_map/ppermute | solution.py:13
  57.3 57.6 %copy-start.1 = (bf16[512,3,1024]{2,0,1:T(8,128)(2,1)S(1)}, bf16[512,3,1024]{2,0,1:T(8,128)(2,1)}, u32[]{:S(2)}) copy-start(bf16[512,3,1024]{2,0,1:T(8,128)(2,1)} %all-gather.2.cloned.1.call-done) | copy-start | bytes 9437188
  57.3 108.6 %all-reduce.3.cloned.1.call-start = ((), (), s32[]{:S(2)}) async-start(), calls=%async_computation.5 | async-start | bytes 1835008 | tf_op jit(solution)/shard_map/psum | solution.py:105
  82.2 36.7 %collective-permute-start.3 = (bf16[512,1024]{1,0:T(8,128)(2,1)}, bf16[512,1024]{1,0:T(8,128)(2,1)}, u32[]{:S(2)}, u32[]{:S(2)}) collective-permute-start(bf16[512,1024]{1,0:T(8,128)(2,1)} %collective-permute-done.2), channel_id=1, source_target_pairs={{4,0},{8,4},{12,8},{5,1},{9,5},{13,9},{6,2},{10,6},{14,10},{7,3},{... | collective-permute-start | bytes 3145736 | tf_op jit(solution)/shard_map/ppermute | solution.py:13
  116.8 2.1 %copy-start.12 = (bf16[1,512,512]{2,1,0:T(8,128)(2,1)S(1)}, bf16[1,512,512]{2,1,0:T(8,128)(2,1)}, u32[]{:S(2)}) copy-start(bf16[1,512,512]{2,1,0:T(8,128)(2,1)} %param.7) | copy-start | bytes 1572868
  167.2 1.6 copy-start.9
Sparse Core Ops, SparseCore 0:
  9.6 31.2 all-gather.1
  52.5 37.9 reduce-scatter.6
  93.2 21.6 reduce-scatter.4
  117.7 48.1 all-reduce.2
where the time goes:
time: 177 us; the launch traced here: 176 us
  waiting for transfers between devices  113 us (64%)
  matrix products  18.3 us (10%)
  between operations  14 us (8%)
  starting transfers between devices  12 us (7%)
  local copies, waits for them, and re-layouts  8.45 us (5%)
  blocking collectives  7.38 us (4%)
  other arithmetic  3.45 us (2%)
    psum x1, waiting for transfers between devices, local(): lax.psum(conv_share, 'seq').astype(jnp.float32)  44.2 us
    ppermute x4, waiting for transfers between devices, passed_along(): return lax.ppermute(block, axis, route)  28.9 us
    reduce_scatter x1, waiting for transfers between devices, local(): lax.psum_scatter(lax.dot_general(gated, upstream, outer, preferred_elemen...  22.1 us
    all_gather x1, waiting for transfers between devices, local(): full_conv = lax.all_gather(conv_weight, ('dp', 'sub'), axis=0, tiled=True)  12.2 us
    ppermute x4, starting transfers between devices, passed_along(): return lax.ppermute(block, axis, route)  11.8 us
    unnamed x29, local copies, waits for them, and re-layouts  8.45 us
    all_gather x1, blocking collectives, local(): full_proj = lax.all_gather(proj_weight, ('dp', 'sub'), axis=0, tiled=True)  7.38 us
    unnamed x5, waiting for transfers between devices  5.17 us
  transfers between devices with their start and end apart: 8, of which 6 were waited for; matrix products, arithmetic and copies ran while one was open for 10% of the time, Pallas kernels for 0%

commit v1 on v0

--- a/solution.py
+++ b/solution.py
@@ -102,7 +102,7 @@
         tiled=True,
     )
     conv_total, proj_total = (
-        lax.psum(conv_share, "seq").astype(jnp.float32),
+        jnp.sum(lax.all_gather(conv_share, "seq"), axis=0).astype(jnp.float32),
         lax.psum(proj_share, "seq").astype(jnp.float32),
     )
     all_rows = row_count * lax.axis_size("seq") * lax.axis_size(("dp", "sub"))

time: 177 us -> 243 us (1.37)
  waiting for transfers between devices: 113 us -> 169 us
  other arithmetic: 3.45 us -> 9.86 us
  local copies, waits for them, and re-layouts: 8.45 us -> 12 us
    psum x1, waiting for transfers between devices: 44.2 us -> 0.01 us  [local(): lax.psum(proj_share, 'seq').astype(jnp.float32)]
    ppermute x4, waiting for transfers between devices: 28.9 us -> 71.9 us  [passed_along(): return lax.ppermute(block, axis, route)]
    unnamed x5 -> x6, waiting for transfers between devices: 5.17 us -> 41.4 us
    all_gather x0 -> x1, waiting for transfers between devices: none -> 27.7 us  [local(): lax.all_gather(conv_share, 'seq')]
    reduce_scatter x1, waiting for transfers between devices: 22.1 us -> 16 us  [local(): lax.psum_scatter(lax.dot_general(gated, upstream, outer, preferred_elemen...]
    reduce_sum x0 -> x1, other arithmetic: none -> 5.18 us  [local(): jnp.sum(lax.all_gather(conv_share, 'seq'), axis=0).astype(jnp.float32)]
    all_gather x0 -> x1, local copies, waits for them, and re-layouts: none -> 3.75 us  [local(): lax.all_gather(conv_share, 'seq')]
    unnamed x29 -> x23, local copies, waits for them, and re-layouts: 8.45 us -> 8.2 us
  transfers between devices with their start and end apart: 8 -> 9, of which waited for: 6 -> 7; matrix products, arithmetic and copies ran while one was open for 10% -> 10% of each run, Pallas kernels for 0% -> 0%
where the time goes in v1:
time: 243 us; the launch traced here: 242 us
  waiting for transfers between devices  169 us (70%)
  matrix products  17.6 us (7%)
  between operations  14 us (6%)
  starting transfers between devices  12.3 us (5%)
  local copies, waits for them, and re-layouts  12 us (5%)
  other arithmetic  9.86 us (4%)
  blocking collectives  7.38 us (3%)
    ppermute x4, waiting for transfers between devices, passed_along(): return lax.ppermute(block, axis, route)  71.9 us
    unnamed x6, waiting for transfers between devices  41.4 us
    all_gather x1, waiting for transfers between devices, local(): lax.all_gather(conv_share, 'seq')  27.7 us
    reduce_scatter x1, waiting for transfers between devices, local(): lax.psum_scatter(lax.dot_general(gated, upstream, outer, preferred_elemen...  16 us
    all_gather x1, waiting for transfers between devices, local(): full_conv = lax.all_gather(conv_weight, ('dp', 'sub'), axis=0, tiled=True)  12.2 us
    ppermute x4, starting transfers between devices, passed_along(): return lax.ppermute(block, axis, route)  12.1 us
    unnamed x23, local copies, waits for them, and re-layouts  8.2 us
    all_gather x1, blocking collectives, local(): full_proj = lax.all_gather(proj_weight, ('dp', 'sub'), axis=0, tiled=True)  7.38 us
  transfers between devices with their start and end apart: 9, of which 7 were waited for; matrix products, arithmetic and copies ran while one was open for 10% of the time, Pallas kernels for 0%

profile of v1, /device:TPU:0, one launch (start us, length us, event | category | flops | bytes accessed | tf_op | source)
XLA Modules:
  0.0 242.3 jit_solution(13397818497920763570)
XLA Ops:
  7.2 0.0 all-gather.4.cloned.1.call-start
  7.2 0.7 all-gather.4.cloned.1.call-update
  7.9 0.0 reduce-scatter.5.cloned.1.call-start
  7.9 5.0 %collective-permute-start = (bf16[512,512]{1,0:T(8,128)(2,1)}, bf16[512,512]{1,0:T(8,128)(2,1)S(1)}, u32[]{:S(2)}, u32[]{:S(2)}) collective-permute-start(bf16[512,512]{1,0:T(8,128)(2,1)} %bitcast.59), channel_id=1, source_target_pairs={{0,4},{4,8},{8,12},{1,5},{5,9},{9,13},{2,6},{6,10},{10,14},{3,7},{... | collective-permute-start | bytes 1572872 | tf_op jit(solution)/shard_map/ppermute | solution.py:13
  12.9 7.4 %all_gather.15 = bf16[512,512]{1,0:T(8,128)(2,1)S(1)} all-gather(bf16[128,512]{1,0:T(8,128)(2,1)} %param.6), channel_id=1, replica_groups=mesh['groups'=2,'seq'=4,'dp'=2,'sub'=2] {'dp','sub'}, dimensions={0}, use_global_device_ids=true | all-gather | bytes 655360 | tf_op jit(solution)/shard_map/all_gather | solution.py:41
  20.3 0.0 copy-start.3
  20.3 4.1 %collective-permute-done = bf16[512,512]{1,0:T(8,128)(2,1)S(1)} collective-permute-done((bf16[512,512]{1,0:T(8,128)(2,1)}, bf16[512,512]{1,0:T(8,128)(2,1)S(1)}, u32[]{:S(2)}, u32[]{:S(2)}) %collective-permute-start) | collective-permute-done | bytes 524320 | tf_op jit(solution)/shard_map/ppermute | solution.py:13
  24.4 4.3 %collective-permute-start.1 = (bf16[512,512]{1,0:T(8,128)(2,1)S(1)}, bf16[512,512]{1,0:T(8,128)(2,1)S(1)}, u32[]{:S(2)}, u32[]{:S(2)}) collective-permute-start(bf16[512,512]{1,0:T(8,128)(2,1)S(1)} %collective-permute-done), channel_id=1, source_target_pairs={{0,4},{4,8},{8,12},{1,5},{5,9},{9,13},{2,6},{6,10},{10,14},{3,7},{... | collective-permute-start | bytes 1572872 | tf_op jit(solution)/shard_map/ppermute | solution.py:13
  28.7 12.2 %all-gather.4.cloned.1.call-done = bf16[512,3,1024]{2,0,1:T(8,128)(2,1)} async-done(((bf16[128,3,1024]{2,0,1:T(8,128)(2,1)}), bf16[512,3,1024]{2,0,1:T(8,128)(2,1)}) %all-gather.4.cloned.1.call-update) | async-done | bytes 3145744 | tf_op jit(solution)/shard_map/all_gather | solution.py:40
  40.8 0.0 copy-start
  40.8 2.2 fusion.12
  43.1 0.1 copy-done
  43.2 0.7 fusion.13
  43.9 0.0 copy-start.9
  43.9 0.0 collective-permute-done.1
  43.9 0.8 add_add_fusion
  44.7 0.0 copy-done.3
  44.7 0.2 copy-done.9
  45.0 0.9 multiply_convert_fusion.1
  45.9 0.0 copy-start.8
  45.9 0.0 copy-start.4
  45.9 0.0 copy-start.6
  45.9 0.0 copy-start.2
  45.9 0.8 copy-done.8
  46.7 1.3 convolution_convert_fusion.3
  47.9 0.0 reduce-scatter.5.cloned.1.call-update
  48.0 0.0 reduce-scatter.7.cloned.1.call-start
  48.0 0.0 copy-done.2
  48.0 0.7 fusion.1
  48.8 0.7 fusion.3
  49.5 0.0 copy-done.4
  49.5 0.0 copy-done.6
  49.5 0.7 fusion.2
  50.3 0.3 pad_maximum_fusion
  50.6 3.1 %copy.16 = bf16[512,3072]{1,0:T(8,128)(2,1)} copy(bf16[512,3072]{0,1:T(8,128)(2,1)S(1)} %bitcast.57) | data formatting | bytes 6291456
  53.7 0.0 reduce-scatter.7.cloned.1.call-update
  53.7 0.0 all-reduce.2.cloned.1.call-start
  53.8 16.0 %reduce-scatter.5.cloned.1.call-done = bf16[128,512]{1,0:T(8,128)(2,1)} async-done(((bf16[512,512]{1,0:T(8,128)(2,1)}), bf16[128,512]{1,0:T(8,128)(2,1)}) %reduce-scatter.5.cloned.1.call-update) | async-done | bytes 131088 | tf_op jit(solution)/shard_map/reduce_scatter | solution.py:96
  69.8 0.0 all-reduce.2.cloned.1.call-update
  69.8 0.0 all-gather.6.cloned.1.call-start
  69.8 40.6 %reduce-scatter.7.cloned.1.call-done = bf16[128,3072]{1,0:T(8,128)(2,1)} async-done(((bf16[512,3072]{1,0:T(8,128)(2,1)}), bf16[128,3072]{1,0:T(8,128)(2,1)}) %reduce-scatter.7.cloned.1.call-update) | async-done | bytes 786448
  110.4 2.4 copy.17
  112.8 0.0 all-gather.6.cloned.1.call-update
  112.8 0.0 copy-start.1
  112.9 0.0 copy-start.5
  112.9 0.0 copy-start.7
  112.9 1.4 pad_maximum_fusion.1
  114.3 1.4 collective-permute-start.2
  115.8 29.4 %collective-permute-done.2 = bf16[512,1024]{1,0:T(8,128)(2,1)} collective-permute-done((bf16[512,1024]{1,0:T(8,128)(2,1)S(1)}, bf16[512,1024]{1,0:T(8,128)(2,1)}, u32[]{:S(2)}, u32[]{:S(2)}) %collective-permute-start.2) | collective-permute-done | bytes 1048608 | tf_op jit(solution)/shard_map/ppermute | solution.py:13
  145.1 1.5 collective-permute-start.3
  146.6 2.6 %fusion.7 = bf16[1,512,512]{2,1,0:T(8,128)(2,1)} fusion(bf16[512,512]{1,0:T(8,128)(2,1)} %copy-done.8, bf16[512,512]{1,0:T(8,128)(2,1)} %copy-done.3, bf16[1,512,512]{2,1,0:T(8,128)(2,1)} %param.4), kind=kOutput, calls=%fused_computation.17 | convolution fusion | flops 269221888 | bytes 2097152 | tf_op jit(solution)/shard_map/dot_general | solution.py:55
  149.2 0.0 copy-done.1
  149.2 0.0 copy-done.5
  149.2 0.0 copy-done.7
  149.2 0.8 fusion.11
  150.0 2.9 %convolution_add_fusion.1 = f32[512,512]{1,0:T(8,128)} fusion(f32[512,512]{1,0:T(8,128)S(1)} %fusion.11, bf16[512,1024]{1,0:T(8,128)(2,1)} %collective-permute-done.2, bf16[512,3,1024]{2,0,1:T(8,128)(2,1)S(1)} %copy-done.1), kind=kOutput, calls=%fused_computation.8 | convolution fusion | flops 537133056 | bytes 4194304 | tf_op jit(solution)/shard_map/dot_general | solution.py:78
  152.9 1.6 convert_multiply_fusion.1
  154.6 38.4 %collective-permute-done.3 = bf16[512,1024]{1,0:T(8,128)(2,1)} collective-permute-done((bf16[512,1024]{1,0:T(8,128)(2,1)}, bf16[512,1024]{1,0:T(8,128)(2,1)}, u32[]{:S(2)}, u32[]{:S(2)}) %collective-permute-start.3) | collective-permute-done | bytes 1048608 | tf_op jit(solution)/shard_map/ppermute | solution.py:13
  193.0 3.2 %fusion.6 = bf16[1,512,512]{2,1,0:T(8,128)(2,1)} fusion(f32[512,512]{1,0:T(8,128)} %convolution_add_fusion.1, bf16[512,1024]{1,0:T(8,128)(2,1)} %collective-permute-done.3, bf16[512,3,1024]{2,0,1:T(8,128)(2,1)S(1)} %copy-done.1, bf16[1,512,512]{2,1,0:T(8,128)(2,1)} %param.7), kind=kOutput, calls=%fused_computation.16 | convolution fusion | flops 537919488 | bytes 4194304 | tf_op jit(solution)/shard_map/dot_general | solution.py:78
  196.2 27.7 %all-gather.6.cloned.1.call-done = bf16[512,3,1024]{0,2,1:T(8,128)(2,1)} async-done(((bf16[128,3,1024]{0,2,1:T(8,128)(2,1)}), bf16[512,3,1024]{0,2,1:T(8,128)(2,1)}) %all-gather.6.cloned.1.call-update) | async-done | bytes 3145744 | tf_op jit(solution)/shard_map/all_gather | solution.py:105
  223.9 3.8 %reshape.8 = bf16[4,128,3,1024]{1,0,3,2:T(4,128)(2,1)S(1)} reshape(bf16[512,3,1024]{0,2,1:T(8,128)(2,1)} %all-gather.6.cloned.1.call-done) | data formatting | bytes 6291456 | tf_op jit(solution)/shard_map/all_gather | solution.py:105
  227.7 5.2 %reduce_sum.12 = bf16[128,3,1024]{0,2,1:T(8,128)(2,1)} reduce(bf16[4,128,3,1024]{1,0,3,2:T(4,128)(2,1)S(1)} %reshape.8, bf16[]{:T(256)} %constant.1.clone.1), dimensions={0}, to_apply=%region_1.0 | reduce | flops 1179648 | bytes 3932162 | tf_op jit(solution)/shard_map/reduce_sum | solution.py:105
  232.9 1.3 convert_multiply_fusion
  234.1 1.6 copy.12
  (1 shorter events, 0.0 us)
Async XLA Ops:
  7.2 33.7 %all-gather.4.cloned.1.call-start = ((), (), s32[]{:S(2)}) async-start(), calls=%async_computation.2 | async-start | bytes 3932160 | tf_op jit(solution)/shard_map/all_gather | solution.py:40
  7.9 61.9 %reduce-scatter.5.cloned.1.call-start = ((), (), s32[]{:S(2)}) async-start(), calls=%async_computation.3 | async-start | bytes 655360 | tf_op jit(solution)/shard_map/reduce_scatter | solution.py:96
  7.9 16.4 %collective-permute-start = (bf16[512,512]{1,0:T(8,128)(2,1)}, bf16[512,512]{1,0:T(8,128)(2,1)S(1)}, u32[]{:S(2)}, u32[]{:S(2)}) collective-permute-start(bf16[512,512]{1,0:T(8,128)(2,1)} %bitcast.59), channel_id=1, source_target_pairs={{0,4},{4,8},{8,12},{1,5},{5,9},{9,13},{2,6},{6,10},{10,14},{3,7},{... | collective-permute-start | bytes 1572872 | tf_op jit(solution)/shard_map/ppermute | solution.py:13
  20.3 24.4 %copy-start.3 = (bf16[512,512]{1,0:T(8,128)(2,1)}, bf16[512,512]{1,0:T(8,128)(2,1)S(1)}, u32[]{:S(2)}) copy-start(bf16[512,512]{1,0:T(8,128)(2,1)S(1)} %all_gather.15) | copy-start | bytes 1572868
  24.4 19.6 %collective-permute-start.1 = (bf16[512,512]{1,0:T(8,128)(2,1)S(1)}, bf16[512,512]{1,0:T(8,128)(2,1)S(1)}, u32[]{:S(2)}, u32[]{:S(2)}) collective-permute-start(bf16[512,512]{1,0:T(8,128)(2,1)S(1)} %collective-permute-done), channel_id=1, source_target_pairs={{0,4},{4,8},{8,12},{1,5},{5,9},{9,13},{2,6},{6,10},{10,14},{3,7},{... | collective-permute-start | bytes 1572872 | tf_op jit(solution)/shard_map/ppermute | solution.py:13
  40.8 2.4 copy-start
  43.9 1.0 copy-start.9
  45.9 0.8 copy-start.8
  45.9 3.6 %copy-start.4 = (bf16[512,512]{1,0:T(8,128)(2,1)}, bf16[512,512]{1,0:T(8,128)(2,1)S(1)}, u32[]{:S(2)}) copy-start(bf16[512,512]{1,0:T(8,128)(2,1)S(1)} %get-tuple-element.8) | copy-start | bytes 1572868
  45.9 3.6 %copy-start.6 = (bf16[512,512]{1,0:T(8,128)(2,1)}, bf16[512,512]{1,0:T(8,128)(2,1)S(1)}, u32[]{:S(2)}) copy-start(bf16[512,512]{1,0:T(8,128)(2,1)S(1)} %get-tuple-element.9) | copy-start | bytes 1572868
  45.9 2.1 copy-start.2
  48.0 62.5 %reduce-scatter.7.cloned.1.call-start = ((), (), s32[]{:S(2)}) async-start(), calls=%async_computation.6 | async-start | bytes 3932160
  53.7 99.2 %all-reduce.2.cloned.1.call-start = ((), (), s32[]{:S(2)}) async-start(), calls=%async_computation.4 | async-start | bytes 262144 | tf_op jit(solution)/shard_map/psum | solution.py:106
  69.8 154.2 %all-gather.6.cloned.1.call-start = ((), (), s32[]{:S(2)}) async-start(), calls=%async_computation.5 | async-start | bytes 3932160 | tf_op jit(solution)/shard_map/all_gather | solution.py:105
  112.8 36.4 %copy-start.1 = (bf16[512,3,1024]{2,0,1:T(8,128)(2,1)S(1)}, bf16[512,3,1024]{2,0,1:T(8,128)(2,1)}, u32[]{:S(2)}) copy-start(bf16[512,3,1024]{2,0,1:T(8,128)(2,1)} %all-gather.4.cloned.1.call-done) | copy-start | bytes 9437188
  112.9 36.4 %copy-start.5 = (bf16[512,512]{1,0:T(8,128)(2,1)S(1)}, bf16[512,512]{1,0:T(8,128)(2,1)}, u32[]{:S(2)}) copy-start(bf16[512,512]{1,0:T(8,128)(2,1)} %copy-done.4) | copy-start | bytes 1572868
  112.9 36.4 %copy-start.7 = (bf16[512,512]{1,0:T(8,128)(2,1)S(1)}, bf16[512,512]{1,0:T(8,128)(2,1)}, u32[]{:S(2)}) copy-start(bf16[512,512]{1,0:T(8,128)(2,1)} %copy-done.6) | copy-start | bytes 1572868
  114.3 30.8 %collective-permute-start.2 = (bf16[512,1024]{1,0:T(8,128)(2,1)S(1)}, bf16[512,1024]{1,0:T(8,128)(2,1)}, u32[]{:S(2)}, u32[]{:S(2)}) collective-permute-start(bf16[512,1024]{1,0:T(8,128)(2,1)S(1)} %pad_maximum_fusion.1), channel_id=1, source_target_pairs={{4,0},{8,4},{12,8},{5,1},{9,5},{13,9},{6,2},{10,6},{14,10},{7,3},{... | collective-permute-start | bytes 3145736 | tf_op jit(solution)/shard_map/ppermute | solution.py:13
  145.1 47.9 %collective-permute-start.3 = (bf16[512,1024]{1,0:T(8,128)(2,1)}, bf16[512,1024]{1,0:T(8,128)(2,1)}, u32[]{:S(2)}, u32[]{:S(2)}) collective-permute-start(bf16[512,1024]{1,0:T(8,128)(2,1)} %collective-permute-done.2), channel_id=1, source_target_pairs={{4,0},{8,4},{12,8},{5,1},{9,5},{13,9},{6,2},{10,6},{14,10},{7,3},{... | collective-permute-start | bytes 3145736 | tf_op jit(solution)/shard_map/ppermute | solution.py:13
Sparse Core Ops, SparseCore 0:
  9.6 31.2 all-gather.3
  48.1 21.6 reduce-scatter.4
  72.5 37.9 reduce-scatter.6
  112.6 35.0 all-reduce.1
  149.2 74.7 all-gather.5
